TPU v7x, 32 devices: a whole 2x2x4 slice. The times are simulated.
32 devices in a mesh: shots: 2 (over y), lat: 4 (over z), depth: 4 (over x, core).
Axes of the slice: x: 2, y: 2, z: 4, core: 2. Of those that a mesh axis runs over, the one named last changes fastest.
Arguments:
- source: float32 [8, 32, 1024], P('shots', 'lat'), parts along dimension 0, may hold values from -6 to 6
- traces: float32 [64, 4096], P(('shots', 'lat')), parts along dimension 0, may hold values from -6 to 6
- trace_tiles: int32 [64, 1], P(('shots', 'lat')), parts along dimension 0, may hold values from 0 to 3; in each aligned block of 8 rows (0 to 7, 8 to 15, ...) at most 5 rows name the same one
- trace_offsets: int32 [64], P(('shots', 'lat')), parts along dimension 0, may hold values from 0 to 7
- stencil: float32 [4, 2, 9, 9], replicated, may hold values from -0.9 to 0.9
- angular_freq: float32 [4], replicated, may hold values from 2 to 6
- slowness: float32 [4, 16384], P('depth', 'lat'), may hold values from 0.5 to 2
- reflect: float32 [4, 16384], P('depth', 'lat'), may hold values from -4 to 4
Outputs:
- picture: float32 [8, 16384], P(('shots', 'depth'), 'lat'), parts along dimension 0
- residual: float32 [64, 4, 1024], P(('shots', 'lat', 'depth')), parts along dimension 0
There are 2 independent parts, one for each index of `shots`. A program takes and returns all parts, laid end to end along the dimension named above; an argument that names none is the same for every part. Nothing has to cross between parts.
Inputs may be any that keep to these rules, and one draw needn't show every extreme that they name: `trace_tiles`: among the 8 blocks of one device, at most 5 name the same tile; on some device one tile is named by exactly 5 of them.
All inputs are finite; a program needn't handle non-finite values.
Results may differ from a plain program's by a relative error of at most 0.00029.
Values sent between devices are 32-bit elements; how exact they have to be, the bound alone decides.
A program may use at most 64 MiB of HBM per device.

v0:
```python
import jax
import jax.numpy as jnp
from jax import lax
from jax.sharding import PartitionSpec as P

precision_high = lax.Precision.HIGHEST


def padded_2(array, sides, width):
    for axis, dim in sides:
        count, length = (lax.axis_size(axis), array.shape[dim])
        up = [(i, (i + 1) % count) for i in range(count - 1)]
        down = [(j, i) for i, j in up]
        last = lax.slice_in_dim(array, length - width, length, axis=dim)
        leading = lax.slice_in_dim(array, 0, width, axis=dim)
        before = lax.ppermute(last, axis, up)
        after = lax.ppermute(leading, axis, down)
        array = jnp.concatenate([before, array, after], axis=dim)
    return array


def from_behind(value, axis, steps):
    count = lax.axis_size(axis)
    leading, last = (max(0, -steps), min(count, count - steps))
    return lax.ppermute(value, axis, [(source, source + steps) for source in range(leading, last)])


def broadcast(block, axis, holder):
    block = jnp.where(lax.axis_index(axis) == holder, block, jnp.zeros_like(block))
    return lax.psum(block, axis)


def make_taps(stencil):
    adjoint = jnp.stack([stencil[:, 0, ::-1, ::-1], -stencil[:, 1, ::-1, ::-1]], axis=1)
    return (stencil, adjoint)


def rotate(wave_field, phase_angle, direction):
    half_width = phase_angle.shape[-1]
    cosine = jnp.cos(phase_angle)
    sine_part = direction * jnp.sin(phase_angle)
    real_part = wave_field[..., :half_width]
    imag_part = wave_field[..., half_width:]
    return jnp.concatenate(
        [real_part * cosine - imag_part * sine_part, real_part * sine_part + imag_part * cosine],
        axis=-1,
    )


def convolve(wave_field, taps):
    tap_count = taps.shape[-1]
    tap_reach = tap_count // 2
    line_count = wave_field.shape[2]
    half_width = wave_field.shape[3] // 2
    padded = padded_2(wave_field, (("lat", 2),), tap_reach)
    widths = ((0, 0), (0, 0), (0, 0), (tap_reach, tap_reach))
    real_pad = jnp.pad(padded[..., :half_width], widths)
    imag_pad = jnp.pad(padded[..., half_width:], widths)
    out_shape = (wave_field.shape[0], wave_field.shape[1], line_count, half_width)
    out_real = jnp.zeros(out_shape, jnp.float32)
    out_imag = jnp.zeros(out_shape, jnp.float32)
    for row_tap in range(tap_count):
        for col_tap in range(tap_count):
            real_piece = real_pad[
                :, :, row_tap : row_tap + line_count, col_tap : col_tap + half_width
            ]
            imag_piece = imag_pad[
                :, :, row_tap : row_tap + line_count, col_tap : col_tap + half_width
            ]
            tap_real = taps[:, 0, row_tap, col_tap][None, :, None, None]
            tap_imag = taps[:, 1, row_tap, col_tap][None, :, None, None]
            out_real = out_real + tap_real * real_piece - tap_imag * imag_piece
            out_imag = out_imag + tap_imag * real_piece + tap_real * imag_piece
    return jnp.concatenate([out_real, out_imag], axis=-1)


def march_down(wave_field, op_table, angles):
    wave_field = rotate(convolve(wave_field, op_table), angles[0], 1.0)
    stored = [wave_field]
    return jnp.stack(stored)


def march_up(up_wave, op_table, angles, src_levels, model_pair):
    for step_index in reversed(range(angles.shape[0])):
        up_wave = up_wave + model_pair[step_index][None, None] * src_levels[step_index][None]
        up_wave = convolve(rotate(up_wave, angles[step_index], -1.0), op_table)
    return up_wave


def local(source, traces, trace_tiles, trace_offsets, stencil, angular_freq, slowness, reflect):
    freq_count, tile_rows, full_width = source.shape
    half_width = full_width // 2
    step_count = slowness.shape[0]
    depth_count = lax.axis_size("depth")
    depth_index = lax.axis_index("depth")
    forward, adjoint = make_taps(stencil)
    places = jnp.arange(tile_rows).astype(jnp.float32)
    targets = (trace_tiles[:, 0] * tile_rows + trace_offsets).astype(jnp.float32)
    lat_start = (lax.axis_index("lat") * tile_rows).astype(jnp.float32)
    piece_traces = lax.all_gather(traces, "lat", axis=0, tiled=True)
    piece_rows = lax.all_gather(targets, "lat", axis=0, tiled=True)
    selector = ((piece_rows - lat_start)[None, :] == places[:, None]).astype(jnp.float32)
    observed = jnp.dot(selector, piece_traces, precision=precision_high)
    observed = observed.reshape(tile_rows, freq_count, full_width)
    surface = jnp.transpose(observed, (1, 0, 2))
    receiver = jnp.concatenate([surface[..., :half_width], -surface[..., half_width:]], axis=-1)
    pair_fields = jnp.stack([source, receiver])
    level_slow = slowness.reshape(step_count, tile_rows, half_width)
    angles = angular_freq[None, :, None, None] * level_slow[:, None]
    model_half = reflect.reshape(step_count, tile_rows, half_width)
    model_pair = jnp.concatenate([model_half, model_half], axis=-1)
    top_slab = depth_index == 0
    top_input = jnp.where(top_slab, pair_fields, 0.0)

    def round_down(turn_index, current):
        bottom = march_down(current, forward, angles)[-1]
        return from_behind(bottom, "depth", 1) + top_input

    current = lax.fori_loop(0, depth_count - 1, round_down, top_input)
    levels = march_down(current, forward, angles)
    sources = levels[:, 0]

    def round_up(turn_index, current):
        top_field = march_up(current, adjoint, angles, sources, model_pair)
        return from_behind(top_field, "depth", -1)

    below = jnp.zeros((1, freq_count, tile_rows, full_width), jnp.float32)
    current = lax.fori_loop(0, depth_count - 1, round_up, below)
    upward = march_up(current, adjoint, angles, sources, model_pair)
    product = levels[:, 0] * levels[:, 1]
    picture = jnp.sum(product[..., :half_width] - product[..., half_width:], axis=1).reshape(
        step_count, tile_rows * half_width
    )
    surface_up = broadcast(upward[0], "depth", 0)
    row_share = tile_rows // depth_count
    row_start = depth_index * row_share
    own_part = lax.dynamic_slice_in_dim(surface_up, row_start, row_share, 1)
    own_seen = lax.dynamic_slice_in_dim(observed, row_start, row_share, 0)
    residual = jnp.transpose(own_part, (1, 0, 2)) - own_seen
    return (picture, residual)


def solution(mesh):
    in_specs = (
        P("shots", "lat", None),
        P(("shots", "lat"), None),
        P(("shots", "lat"), None),
        P(("shots", "lat")),
        P(),
        P(),
        P("depth", "lat"),
        P("depth", "lat"),
    )
    out_specs = (P(("shots", "depth"), "lat"), P(("shots", "lat", "depth"), None, None))
    return jax.shard_map(local, mesh=mesh, in_specs=in_specs, out_specs=out_specs, check_vma=False)
```

profile of v0, /device:TPU:0, one launch (start us, length us, event | category | flops | bytes accessed | tf_op | source)
XLA Modules:
  0.0 301.9 jit_solution(15912066643965686476)
XLA Ops:
  9.9 13.5 %all-reduce.8 = f32[32]{0:T(128)S(1)} all-reduce(f32[32]{0:T(128)S(1)} %fusion.48), channel_id=1, replica_groups=mesh['shots'=2,'lat'=4,'depth'=4] {'lat'}, use_global_device_ids=true, to_apply=%add.8 | all-reduce | flops 32 | bytes 256
  23.4 15.0 %all_gather.7 = f32[32,4096]{1,0:T(8,128)S(1)} all-gather(f32[8,4096]{1,0:T(8,128)} %param.13), channel_id=1, replica_groups=mesh['shots'=2,'lat'=4,'depth'=4] {'lat'}, dimensions={0}, use_global_device_ids=true | all-gather | bytes 655360 | tf_op jit(solution)/shard_map/all_gather | solution.py:100
  41.7 100.5 %while.28 = (s32[]{:T(128)}, f32[2,4,8,1024]{3,2,1,0:T(8,128)S(1)}, f32[4,2,9,9]{0,3,2,1:T(8,128)S(1)}, f32[2,4,8,1024]{3,2,1,0:T(8,128)S(1)}, f32[8,512]{1,0:T(8,128)S(1)}, /*index=5*/f32[4]{0:T(128)S(1)}, s32[]{:T(128)}) while((s32[]{:T(128)}, f32[2,4,8,1024]{3,2,1,0:T(8,128)S(1)}, f32[4,2,9,9]{0,3,2,1:T(8,128)S(1)}, ...), condition=%wide.region_1.2_spmd.clone.clone, body=%wide.region_0.1_spmd.clone.clone.sunk | while | flops 22265856 | bytes 10328341 | solution.py:119
  41.8 1.3 collective-permute-start
  43.1 4.6 %collective-permute-start.1 = (f32[2,4,4,1024]{3,2,1,0:T(4,128)S(1)}, f32[2,4,4,1024]{3,2,1,0:T(4,128)S(1)}, u32[]{:S(2)}, u32[]{:S(2)}) collective-permute-start(f32[2,4,4,1024]{3,2,1,0:T(4,128)S(1)} %get-tuple-element.1461), channel_id=1, source_target_pairs={{0,4},{4,8},{8,12},{1,5},{5,9},{9,13},{2,6},{6,10},{10,14},{3,7},{... | collective-permute-start | bytes 393224 | tf_op jit(solution)/shard_map/while/body/eval_jaxpr/ppermute | solution.py:16
  48.7 1.5 collective-permute-done.1
  50.3 18.9 %multiply_subtract_fusion.10 = (f32[2,4,8,512]{3,2,1,0:T(8,128)S(1)}, f32[2,4,8,512]{3,2,1,0:T(8,128)S(1)}, f32[2,4,8,512]{3,2,1,0:T(8,128)S(1)}) fusion(f32[4,8,512]{2,1,0:T(8,128)S(1)} %get-tuple-element.1360, f32[4,8,512]{2,1,0:T(8,128)S(1)} %get-tuple-element.1361, f32[4]{0:T(128)S(1)} %get-tuple-element.1362, f32[4]{0:T(128)S(1)} %get-tuple-element.1363, ...), kind=kLoop, calls=%fused_computation.173.clone.1 | loop fusion | flops 21757952 | bytes 2835456 | tf_op jit(solution)/shard_map/while/body/eval_jaxpr/sub | solution.py:45
  69.4 1.3 collective-permute-start.2
  71.9 1.3 collective-permute-start
  73.2 5.0 %collective-permute-start.1 = (f32[2,4,4,1024]{3,2,1,0:T(4,128)S(1)}, f32[2,4,4,1024]{3,2,1,0:T(4,128)S(1)}, u32[]{:S(2)}, u32[]{:S(2)}) collective-permute-start(f32[2,4,4,1024]{3,2,1,0:T(4,128)S(1)} %get-tuple-element.1461), channel_id=1, source_target_pairs={{0,4},{4,8},{8,12},{1,5},{5,9},{9,13},{2,6},{6,10},{10,14},{3,7},{... | collective-permute-start | bytes 393224 | tf_op jit(solution)/shard_map/while/body/eval_jaxpr/ppermute | solution.py:16
  79.2 1.5 collective-permute-done.1
  80.9 18.9 %multiply_subtract_fusion.10 = (f32[2,4,8,512]{3,2,1,0:T(8,128)S(1)}, f32[2,4,8,512]{3,2,1,0:T(8,128)S(1)}, f32[2,4,8,512]{3,2,1,0:T(8,128)S(1)}) fusion(f32[4,8,512]{2,1,0:T(8,128)S(1)} %get-tuple-element.1360, f32[4,8,512]{2,1,0:T(8,128)S(1)} %get-tuple-element.1361, f32[4]{0:T(128)S(1)} %get-tuple-element.1362, f32[4]{0:T(128)S(1)} %get-tuple-element.1363, ...), kind=kLoop, calls=%fused_computation.173.clone.1 | loop fusion | flops 21757952 | bytes 2835456 | tf_op jit(solution)/shard_map/while/body/eval_jaxpr/sub | solution.py:45
  99.9 5.4 %collective-permute-start.2 = (f32[2,4,8,1024]{3,2,1,0:T(8,128)S(1)}, f32[2,4,8,1024]{3,2,1,0:T(8,128)S(1)}, u32[]{:S(2)}, u32[]{:S(2)}) collective-permute-start(f32[2,4,8,1024]{3,2,1,0:T(8,128)S(1)} %pad_maximum_fusion.17), channel_id=1, source_target_pairs={{0,1},{1,2},{2,3},{4,5},{5,6},{6,7},{8,9},{9,10},{10,11},{12,13},{... | collective-permute-start | bytes 786440 | tf_op jit(solution)/shard_map/while/body/eval_jaxpr/ppermute | solution.py:25
  106.6 1.3 collective-permute-start
  107.9 4.7 %collective-permute-start.1 = (f32[2,4,4,1024]{3,2,1,0:T(4,128)S(1)}, f32[2,4,4,1024]{3,2,1,0:T(4,128)S(1)}, u32[]{:S(2)}, u32[]{:S(2)}) collective-permute-start(f32[2,4,4,1024]{3,2,1,0:T(4,128)S(1)} %get-tuple-element.1461), channel_id=1, source_target_pairs={{0,4},{4,8},{8,12},{1,5},{5,9},{9,13},{2,6},{6,10},{10,14},{3,7},{... | collective-permute-start | bytes 393224 | tf_op jit(solution)/shard_map/while/body/eval_jaxpr/ppermute | solution.py:16
  113.6 1.5 collective-permute-done.1
  115.2 18.9 %multiply_subtract_fusion.10 = (f32[2,4,8,512]{3,2,1,0:T(8,128)S(1)}, f32[2,4,8,512]{3,2,1,0:T(8,128)S(1)}, f32[2,4,8,512]{3,2,1,0:T(8,128)S(1)}) fusion(f32[4,8,512]{2,1,0:T(8,128)S(1)} %get-tuple-element.1360, f32[4,8,512]{2,1,0:T(8,128)S(1)} %get-tuple-element.1361, f32[4]{0:T(128)S(1)} %get-tuple-element.1362, f32[4]{0:T(128)S(1)} %get-tuple-element.1363, ...), kind=kLoop, calls=%fused_computation.173.clone.1 | loop fusion | flops 21757952 | bytes 2835456 | tf_op jit(solution)/shard_map/while/body/eval_jaxpr/sub | solution.py:45
  134.3 6.9 %collective-permute-start.2 = (f32[2,4,8,1024]{3,2,1,0:T(8,128)S(1)}, f32[2,4,8,1024]{3,2,1,0:T(8,128)S(1)}, u32[]{:S(2)}, u32[]{:S(2)}) collective-permute-start(f32[2,4,8,1024]{3,2,1,0:T(8,128)S(1)} %pad_maximum_fusion.17), channel_id=1, source_target_pairs={{0,1},{1,2},{2,3},{4,5},{5,6},{6,7},{8,9},{9,10},{10,11},{12,13},{... | collective-permute-start | bytes 786440 | tf_op jit(solution)/shard_map/while/body/eval_jaxpr/ppermute | solution.py:25
  142.3 4.1 %collective-permute-start.6 = (f32[2,4,4,1024]{3,2,1,0:T(4,128)S(1)}, f32[2,4,4,1024]{3,2,1,0:T(4,128)S(1)}, u32[]{:S(2)}, u32[]{:S(2)}) collective-permute-start(f32[2,4,4,1024]{3,2,1,0:T(4,128)S(1)} %get-tuple-element.844), channel_id=1, source_target_pairs={{0,4},{4,8},{8,12},{1,5},{5,9},{9,13},{2,6},{6,10},{10,14},{3,7},{... | collective-permute-start | bytes 393224 | tf_op jit(solution)/shard_map/ppermute | solution.py:16
  146.4 1.3 collective-permute-start.7
  151.7 1.6 collective-permute-done.7
  153.5 19.0 %multiply_subtract_fusion.3 = (f32[2,4,8,512]{3,2,1,0:T(8,128)S(1)}, f32[2,4,8,512]{3,2,1,0:T(8,128)S(1)}, f32[2,4,8,512]{3,2,1,0:T(8,128)S(1)}) fusion(f32[4,8,512]{2,1,0:T(8,128)S(1)} %get-tuple-element.938, f32[4,8,512]{2,1,0:T(8,128)S(1)} %get-tuple-element.937, f32[4]{0:T(128)S(1)} %get-tuple-element.426, f32[4]{0:T(128)S(1)} %get-tuple-element.425, ...), kind=kLoop, calls=%fused_computation.1000 | loop fusion | flops 21757952 | bytes 2835456 | tf_op jit(solution)/shard_map/sub | solution.py:45
  172.5 72.3 %while.29 = (s32[]{:T(128)}, f32[1,4,8,1024]{3,2,1,0:T(8,128)S(1)}, f32[4,1,9,9]{0,3,2,1:T(8,128)S(1)}, f32[1,8,1024]{2,1,0:T(8,128)S(1)}, f32[1,4,8,1024]{3,2,1...) while((s32[]{:T(128)}, f32[1,4,8,1024]{3,2,1,0:T(8,128)S(1)}, ...), condition=%wide.region_4.5_spmd.clone.clone, body=%wide.region_3.4_spmd.clone.clone.sunk | while | flops 11239426 | bytes 7006565 | solution.py:128
  172.9 3.9 %collective-permute-start.3 = (f32[1,4,4,1024]{3,2,1,0:T(4,128)S(1)}, f32[1,4,4,1024]{3,2,1,0:T(4,128)S(1)}, u32[]{:S(2)}, u32[]{:S(2)}) collective-permute-start(f32[1,4,4,1024]{3,2,1,0:T(4,128)S(1)} %get-tuple-element.1541), channel_id=1, source_target_pairs={{0,4},{4,8},{8,12},{1,5},{5,9},{9,13},{2,6},{6,10},{10,14},{3,7},{... | collective-permute-start | bytes 196616 | tf_op jit(solution)/shard_map/while/body/eval_jaxpr/ppermute | solution.py:16
  176.9 1.3 collective-permute-start.4
  178.7 4.3 %collective-permute-done.4 = f32[1,4,4,1024]{3,2,1,0:T(4,128)S(1)} collective-permute-done((f32[1,4,4,1024]{3,2,1,0:T(4,128)S(1)}, f32[1,4,4,1024]{3,2,1,0:T(4,128)S(1)}, u32[]{:S(2)}, u32[]{:S(2)}) %collective-permute-start.4) | collective-permute-done | bytes 65568 | tf_op jit(solution)/shard_map/while/body/eval_jaxpr/ppermute | solution.py:17
  183.2 3.7 %multiply_subtract_fusion.11 = f32[1,4,8,512]{3,2,1,0:T(8,128)S(1)} fusion(f32[1,4,8,512]{3,2,1,0:T(8,128)S(1)} %get-tuple-element.1539, f32[1,4,8,512]{3,2,1,0:T(8,128)S(1)} %get-tuple-element.1540, f32[1,4,12,1024]{3,2,1,0:T(8,128)S(1)} %get-tuple-element.1543, f32[1,4,12,1024]{3,2,1,0:T(8,128)S(1)} %get-tuple-element.1544, ...), kind=kLoop, calls=%fused_computation.510.clone.1 | loop fusion | flops 5292032 | bytes 1509920 | tf_op jit(solution)/shard_map/while/body/eval_jaxpr/sub | solution.py:72
  186.8 3.7 %multiply_add_fusion.21 = f32[1,4,8,512]{3,2,1,0:T(8,128)S(1)} fusion(f32[1,4,8,512]{3,2,1,0:T(8,128)S(1)} %get-tuple-element.1539, f32[1,4,8,512]{3,2,1,0:T(8,128)S(1)} %get-tuple-element.1540, f32[1,4,12,1024]{3,2,1,0:T(8,128)S(1)} %get-tuple-element.1543, f32[1,4,12,1024]{3,2,1,0:T(8,128)S(1)} %get-tuple-element.1544, ...), kind=kLoop, calls=%fused_computation.508.clone.1 | loop fusion | flops 5292032 | bytes 1509920 | tf_op jit(solution)/shard_map/while/body/eval_jaxpr/add | solution.py:73
  190.5 1.3 collective-permute-start.5
  191.8 4.9 %collective-permute-done.5 = f32[1,4,8,1024]{3,2,1,0:T(8,128)S(1)} collective-permute-done((f32[1,4,8,1024]{3,2,1,0:T(8,128)S(1)}, f32[1,4,8,1024]{3,2,1,0:T(8,128)S(1)}, u32[]{:S(2)}, u32[]{:S(2)}) %collective-permute-start.5) | collective-permute-done | bytes 131104 | tf_op jit(solution)/shard_map/while/body/eval_jaxpr/ppermute | solution.py:25
  197.1 3.6 %collective-permute-start.3 = (f32[1,4,4,1024]{3,2,1,0:T(4,128)S(1)}, f32[1,4,4,1024]{3,2,1,0:T(4,128)S(1)}, u32[]{:S(2)}, u32[]{:S(2)}) collective-permute-start(f32[1,4,4,1024]{3,2,1,0:T(4,128)S(1)} %get-tuple-element.1541), channel_id=1, source_target_pairs={{0,4},{4,8},{8,12},{1,5},{5,9},{9,13},{2,6},{6,10},{10,14},{3,7},{... | collective-permute-start | bytes 196616 | tf_op jit(solution)/shard_map/while/body/eval_jaxpr/ppermute | solution.py:16
  200.7 1.3 collective-permute-start.4
  202.6 4.3 %collective-permute-done.4 = f32[1,4,4,1024]{3,2,1,0:T(4,128)S(1)} collective-permute-done((f32[1,4,4,1024]{3,2,1,0:T(4,128)S(1)}, f32[1,4,4,1024]{3,2,1,0:T(4,128)S(1)}, u32[]{:S(2)}, u32[]{:S(2)}) %collective-permute-start.4) | collective-permute-done | bytes 65568 | tf_op jit(solution)/shard_map/while/body/eval_jaxpr/ppermute | solution.py:17
  207.0 3.7 %multiply_subtract_fusion.11 = f32[1,4,8,512]{3,2,1,0:T(8,128)S(1)} fusion(f32[1,4,8,512]{3,2,1,0:T(8,128)S(1)} %get-tuple-element.1539, f32[1,4,8,512]{3,2,1,0:T(8,128)S(1)} %get-tuple-element.1540, f32[1,4,12,1024]{3,2,1,0:T(8,128)S(1)} %get-tuple-element.1543, f32[1,4,12,1024]{3,2,1,0:T(8,128)S(1)} %get-tuple-element.1544, ...), kind=kLoop, calls=%fused_computation.510.clone.1 | loop fusion | flops 5292032 | bytes 1509920 | tf_op jit(solution)/shard_map/while/body/eval_jaxpr/sub | solution.py:72
  210.7 3.7 %multiply_add_fusion.21 = f32[1,4,8,512]{3,2,1,0:T(8,128)S(1)} fusion(f32[1,4,8,512]{3,2,1,0:T(8,128)S(1)} %get-tuple-element.1539, f32[1,4,8,512]{3,2,1,0:T(8,128)S(1)} %get-tuple-element.1540, f32[1,4,12,1024]{3,2,1,0:T(8,128)S(1)} %get-tuple-element.1543, f32[1,4,12,1024]{3,2,1,0:T(8,128)S(1)} %get-tuple-element.1544, ...), kind=kLoop, calls=%fused_computation.508.clone.1 | loop fusion | flops 5292032 | bytes 1509920 | tf_op jit(solution)/shard_map/while/body/eval_jaxpr/add | solution.py:73
  214.4 1.3 collective-permute-start.5
  215.7 6.9 %collective-permute-done.5 = f32[1,4,8,1024]{3,2,1,0:T(8,128)S(1)} collective-permute-done((f32[1,4,8,1024]{3,2,1,0:T(8,128)S(1)}, f32[1,4,8,1024]{3,2,1,0:T(8,128)S(1)}, u32[]{:S(2)}, u32[]{:S(2)}) %collective-permute-start.5) | collective-permute-done | bytes 131104 | tf_op jit(solution)/shard_map/while/body/eval_jaxpr/ppermute | solution.py:25
  223.0 3.3 %collective-permute-start.3 = (f32[1,4,4,1024]{3,2,1,0:T(4,128)S(1)}, f32[1,4,4,1024]{3,2,1,0:T(4,128)S(1)}, u32[]{:S(2)}, u32[]{:S(2)}) collective-permute-start(f32[1,4,4,1024]{3,2,1,0:T(4,128)S(1)} %get-tuple-element.1541), channel_id=1, source_target_pairs={{0,4},{4,8},{8,12},{1,5},{5,9},{9,13},{2,6},{6,10},{10,14},{3,7},{... | collective-permute-start | bytes 196616 | tf_op jit(solution)/shard_map/while/body/eval_jaxpr/ppermute | solution.py:16
  228.2 4.3 %collective-permute-done.4 = f32[1,4,4,1024]{3,2,1,0:T(4,128)S(1)} collective-permute-done((f32[1,4,4,1024]{3,2,1,0:T(4,128)S(1)}, f32[1,4,4,1024]{3,2,1,0:T(4,128)S(1)}, u32[]{:S(2)}, u32[]{:S(2)}) %collective-permute-start.4) | collective-permute-done | bytes 65568 | tf_op jit(solution)/shard_map/while/body/eval_jaxpr/ppermute | solution.py:17
  232.6 3.7 %multiply_subtract_fusion.11 = f32[1,4,8,512]{3,2,1,0:T(8,128)S(1)} fusion(f32[1,4,8,512]{3,2,1,0:T(8,128)S(1)} %get-tuple-element.1539, f32[1,4,8,512]{3,2,1,0:T(8,128)S(1)} %get-tuple-element.1540, f32[1,4,12,1024]{3,2,1,0:T(8,128)S(1)} %get-tuple-element.1543, f32[1,4,12,1024]{3,2,1,0:T(8,128)S(1)} %get-tuple-element.1544, ...), kind=kLoop, calls=%fused_computation.510.clone.1 | loop fusion | flops 5292032 | bytes 1509920 | tf_op jit(solution)/shard_map/while/body/eval_jaxpr/sub | solution.py:72
  236.3 3.7 %multiply_add_fusion.21 = f32[1,4,8,512]{3,2,1,0:T(8,128)S(1)} fusion(f32[1,4,8,512]{3,2,1,0:T(8,128)S(1)} %get-tuple-element.1539, f32[1,4,8,512]{3,2,1,0:T(8,128)S(1)} %get-tuple-element.1540, f32[1,4,12,1024]{3,2,1,0:T(8,128)S(1)} %get-tuple-element.1543, f32[1,4,12,1024]{3,2,1,0:T(8,128)S(1)} %get-tuple-element.1544, ...), kind=kLoop, calls=%fused_computation.508.clone.1 | loop fusion | flops 5292032 | bytes 1509920 | tf_op jit(solution)/shard_map/while/body/eval_jaxpr/add | solution.py:73
  241.2 3.6 %collective-permute-done.5 = f32[1,4,8,1024]{3,2,1,0:T(8,128)S(1)} collective-permute-done((f32[1,4,8,1024]{3,2,1,0:T(8,128)S(1)}, f32[1,4,8,1024]{3,2,1,0:T(8,128)S(1)}, u32[]{:S(2)}, u32[]{:S(2)}) %collective-permute-start.5) | collective-permute-done | bytes 131104 | tf_op jit(solution)/shard_map/while/body/eval_jaxpr/ppermute | solution.py:25
  245.2 2.4 collective-permute-start.8
  247.6 1.3 collective-permute-start.9
  249.3 4.5 %collective-permute-done.9 = f32[1,4,4,1024]{3,2,1,0:T(4,128)S(1)} collective-permute-done((f32[1,4,4,1024]{3,2,1,0:T(4,128)S(1)}, f32[1,4,4,1024]{3,2,1,0:T(4,128)S(1)}, u32[]{:S(2)}, u32[]{:S(2)}) %collective-permute-start.9) | collective-permute-done | bytes 65568 | tf_op jit(solution)/shard_map/ppermute | solution.py:17
  253.9 3.7 %multiply_subtract_fusion.5 = f32[1,4,8,512]{3,2,1,0:T(8,128)S(1)} fusion(f32[1,4,8,512]{3,2,1,0:T(8,128)S(1)} %get-tuple-element.847, f32[1,4,8,512]{3,2,1,0:T(8,128)S(1)} %get-tuple-element.846, f32[1,4,12,1024]{3,2,1,0:T(8,128)S(1)} %get-tuple-element.851, f32[1,4,12,1024]{3,2,1,0:T(8,128)S(1)} %get-tuple-element.850, ...), kind=kLoop, calls=%fused_computation.1023 | loop fusion | flops 5292032 | bytes 1509920 | tf_op jit(solution)/shard_map/sub | solution.py:72
  257.5 3.7 %multiply_add_fusion.13 = f32[1,4,8,512]{3,2,1,0:T(8,128)S(1)} fusion(f32[1,4,8,512]{3,2,1,0:T(8,128)S(1)} %get-tuple-element.847, f32[1,4,8,512]{3,2,1,0:T(8,128)S(1)} %get-tuple-element.846, f32[1,4,12,1024]{3,2,1,0:T(8,128)S(1)} %get-tuple-element.851, f32[1,4,12,1024]{3,2,1,0:T(8,128)S(1)} %get-tuple-element.850, ...), kind=kLoop, calls=%fused_computation.1021 | loop fusion | flops 5292032 | bytes 1509920 | tf_op jit(solution)/shard_map/add | solution.py:73
  262.5 30.9 %all-reduce.11.cloned.1.call-done = f32[4,8,1024]{2,1,0:T(8,128)} async-done(((f32[4,8,1024]{2,1,0:T(8,128)}), f32[4,8,1024]{2,1,0:T(8,128)}) %all-reduce.11.cloned.1.call-update) | async-done | bytes 131088 | tf_op jit(solution)/shard_map/psum | solution.py:30
  (187 shorter events, 25.9 us)
Async XLA Ops:
  7.2 286.3 %all-reduce.11.cloned.1.call-start = ((), (), s32[]{:S(2)}) async-start(), calls=%async_computation | async-start | bytes 262144 | tf_op jit(solution)/shard_map/psum | solution.py:30
  7.2 0.7 copy-start.7
  9.1 0.7 copy-start.5
  9.1 0.7 copy-start.6
  38.7 0.9 copy-start.1
  39.7 0.7 copy-start.4
  39.7 1.4 copy-start
  41.1 0.7 copy-start.2
  41.8 6.9 %collective-permute-start = (f32[2,4,4,1024]{3,2,1,0:T(4,128)S(1)}, f32[2,4,4,1024]{3,2,1,0:T(4,128)S(1)}, u32[]{:S(2)}, u32[]{:S(2)}) collective-permute-start(f32[2,4,4,1024]{3,2,1,0:T(4,128)S(1)} %get-tuple-element.1370), channel_id=1, source_target_pairs={{4,0},{8,4},{12,8},{5,1},{9,5},{13,9},{6,2},{10,6},{14,10},{7,3},{... | collective-permute-start | bytes 393224 | tf_op jit(solution)/shard_map/while/body/eval_jaxpr/ppermute | solution.py:17
  43.1 7.1 %collective-permute-start.1 = (f32[2,4,4,1024]{3,2,1,0:T(4,128)S(1)}, f32[2,4,4,1024]{3,2,1,0:T(4,128)S(1)}, u32[]{:S(2)}, u32[]{:S(2)}) collective-permute-start(f32[2,4,4,1024]{3,2,1,0:T(4,128)S(1)} %get-tuple-element.1461), channel_id=1, source_target_pairs={{0,4},{4,8},{8,12},{1,5},{5,9},{9,13},{2,6},{6,10},{10,14},{3,7},{... | collective-permute-start | bytes 393224 | tf_op jit(solution)/shard_map/while/body/eval_jaxpr/ppermute | solution.py:16
  69.4 2.4 collective-permute-start.2
  71.9 7.3 %collective-permute-start = (f32[2,4,4,1024]{3,2,1,0:T(4,128)S(1)}, f32[2,4,4,1024]{3,2,1,0:T(4,128)S(1)}, u32[]{:S(2)}, u32[]{:S(2)}) collective-permute-start(f32[2,4,4,1024]{3,2,1,0:T(4,128)S(1)} %get-tuple-element.1370), channel_id=1, source_target_pairs={{4,0},{8,4},{12,8},{5,1},{9,5},{13,9},{6,2},{10,6},{14,10},{7,3},{... | collective-permute-start | bytes 393224 | tf_op jit(solution)/shard_map/while/body/eval_jaxpr/ppermute | solution.py:17
  73.2 7.5 %collective-permute-start.1 = (f32[2,4,4,1024]{3,2,1,0:T(4,128)S(1)}, f32[2,4,4,1024]{3,2,1,0:T(4,128)S(1)}, u32[]{:S(2)}, u32[]{:S(2)}) collective-permute-start(f32[2,4,4,1024]{3,2,1,0:T(4,128)S(1)} %get-tuple-element.1461), channel_id=1, source_target_pairs={{0,4},{4,8},{8,12},{1,5},{5,9},{9,13},{2,6},{6,10},{10,14},{3,7},{... | collective-permute-start | bytes 393224 | tf_op jit(solution)/shard_map/while/body/eval_jaxpr/ppermute | solution.py:16
  99.9 6.6 %collective-permute-start.2 = (f32[2,4,8,1024]{3,2,1,0:T(8,128)S(1)}, f32[2,4,8,1024]{3,2,1,0:T(8,128)S(1)}, u32[]{:S(2)}, u32[]{:S(2)}) collective-permute-start(f32[2,4,8,1024]{3,2,1,0:T(8,128)S(1)} %pad_maximum_fusion.17), channel_id=1, source_target_pairs={{0,1},{1,2},{2,3},{4,5},{5,6},{6,7},{8,9},{9,10},{10,11},{12,13},{... | collective-permute-start | bytes 786440 | tf_op jit(solution)/shard_map/while/body/eval_jaxpr/ppermute | solution.py:25
  106.6 7.0 %collective-permute-start = (f32[2,4,4,1024]{3,2,1,0:T(4,128)S(1)}, f32[2,4,4,1024]{3,2,1,0:T(4,128)S(1)}, u32[]{:S(2)}, u32[]{:S(2)}) collective-permute-start(f32[2,4,4,1024]{3,2,1,0:T(4,128)S(1)} %get-tuple-element.1370), channel_id=1, source_target_pairs={{4,0},{8,4},{12,8},{5,1},{9,5},{13,9},{6,2},{10,6},{14,10},{7,3},{... | collective-permute-start | bytes 393224 | tf_op jit(solution)/shard_map/while/body/eval_jaxpr/ppermute | solution.py:17
  107.9 7.2 %collective-permute-start.1 = (f32[2,4,4,1024]{3,2,1,0:T(4,128)S(1)}, f32[2,4,4,1024]{3,2,1,0:T(4,128)S(1)}, u32[]{:S(2)}, u32[]{:S(2)}) collective-permute-start(f32[2,4,4,1024]{3,2,1,0:T(4,128)S(1)} %get-tuple-element.1461), channel_id=1, source_target_pairs={{0,4},{4,8},{8,12},{1,5},{5,9},{9,13},{2,6},{6,10},{10,14},{3,7},{... | collective-permute-start | bytes 393224 | tf_op jit(solution)/shard_map/while/body/eval_jaxpr/ppermute | solution.py:16
  134.3 8.0 %collective-permute-start.2 = (f32[2,4,8,1024]{3,2,1,0:T(8,128)S(1)}, f32[2,4,8,1024]{3,2,1,0:T(8,128)S(1)}, u32[]{:S(2)}, u32[]{:S(2)}) collective-permute-start(f32[2,4,8,1024]{3,2,1,0:T(8,128)S(1)} %pad_maximum_fusion.17), channel_id=1, source_target_pairs={{0,1},{1,2},{2,3},{4,5},{5,6},{6,7},{8,9},{9,10},{10,11},{12,13},{... | collective-permute-start | bytes 786440 | tf_op jit(solution)/shard_map/while/body/eval_jaxpr/ppermute | solution.py:25
  142.3 9.4 %collective-permute-start.6 = (f32[2,4,4,1024]{3,2,1,0:T(4,128)S(1)}, f32[2,4,4,1024]{3,2,1,0:T(4,128)S(1)}, u32[]{:S(2)}, u32[]{:S(2)}) collective-permute-start(f32[2,4,4,1024]{3,2,1,0:T(4,128)S(1)} %get-tuple-element.844), channel_id=1, source_target_pairs={{0,4},{4,8},{8,12},{1,5},{5,9},{9,13},{2,6},{6,10},{10,14},{3,7},{... | collective-permute-start | bytes 393224 | tf_op jit(solution)/shard_map/ppermute | solution.py:16
  146.4 6.9 %collective-permute-start.7 = (f32[2,4,4,1024]{3,2,1,0:T(4,128)S(1)}, f32[2,4,4,1024]{3,2,1,0:T(4,128)S(1)}, u32[]{:S(2)}, u32[]{:S(2)}) collective-permute-start(f32[2,4,4,1024]{3,2,1,0:T(4,128)S(1)} %get-tuple-element.845), channel_id=1, source_target_pairs={{4,0},{8,4},{12,8},{5,1},{9,5},{13,9},{6,2},{10,6},{14,10},{7,3},{... | collective-permute-start | bytes 393224 | tf_op jit(solution)/shard_map/ppermute | solution.py:17
  150.7 0.7 copy-start.3
  172.9 5.8 %collective-permute-start.3 = (f32[1,4,4,1024]{3,2,1,0:T(4,128)S(1)}, f32[1,4,4,1024]{3,2,1,0:T(4,128)S(1)}, u32[]{:S(2)}, u32[]{:S(2)}) collective-permute-start(f32[1,4,4,1024]{3,2,1,0:T(4,128)S(1)} %get-tuple-element.1541), channel_id=1, source_target_pairs={{0,4},{4,8},{8,12},{1,5},{5,9},{9,13},{2,6},{6,10},{10,14},{3,7},{... | collective-permute-start | bytes 196616 | tf_op jit(solution)/shard_map/while/body/eval_jaxpr/ppermute | solution.py:16
  176.9 6.2 %collective-permute-start.4 = (f32[1,4,4,1024]{3,2,1,0:T(4,128)S(1)}, f32[1,4,4,1024]{3,2,1,0:T(4,128)S(1)}, u32[]{:S(2)}, u32[]{:S(2)}) collective-permute-start(f32[1,4,4,1024]{3,2,1,0:T(4,128)S(1)} %get-tuple-element.1542), channel_id=1, source_target_pairs={{4,0},{8,4},{12,8},{5,1},{9,5},{13,9},{6,2},{10,6},{14,10},{7,3},{... | collective-permute-start | bytes 196616 | tf_op jit(solution)/shard_map/while/body/eval_jaxpr/ppermute | solution.py:17
  190.5 6.2 %collective-permute-start.5 = (f32[1,4,8,1024]{3,2,1,0:T(8,128)S(1)}, f32[1,4,8,1024]{3,2,1,0:T(8,128)S(1)}, u32[]{:S(2)}, u32[]{:S(2)}) collective-permute-start(f32[1,4,8,1024]{3,2,1,0:T(8,128)S(1)} %pad_maximum_fusion.19), channel_id=1, source_target_pairs={{1,0},{2,1},{3,2},{5,4},{6,5},{7,6},{9,8},{10,9},{11,10},{13,12},{... | collective-permute-start | bytes 393224 | tf_op jit(solution)/shard_map/while/body/eval_jaxpr/ppermute | solution.py:25
  197.1 5.5 %collective-permute-start.3 = (f32[1,4,4,1024]{3,2,1,0:T(4,128)S(1)}, f32[1,4,4,1024]{3,2,1,0:T(4,128)S(1)}, u32[]{:S(2)}, u32[]{:S(2)}) collective-permute-start(f32[1,4,4,1024]{3,2,1,0:T(4,128)S(1)} %get-tuple-element.1541), channel_id=1, source_target_pairs={{0,4},{4,8},{8,12},{1,5},{5,9},{9,13},{2,6},{6,10},{10,14},{3,7},{... | collective-permute-start | bytes 196616 | tf_op jit(solution)/shard_map/while/body/eval_jaxpr/ppermute | solution.py:16
  200.7 6.2 %collective-permute-start.4 = (f32[1,4,4,1024]{3,2,1,0:T(4,128)S(1)}, f32[1,4,4,1024]{3,2,1,0:T(4,128)S(1)}, u32[]{:S(2)}, u32[]{:S(2)}) collective-permute-start(f32[1,4,4,1024]{3,2,1,0:T(4,128)S(1)} %get-tuple-element.1542), channel_id=1, source_target_pairs={{4,0},{8,4},{12,8},{5,1},{9,5},{13,9},{6,2},{10,6},{14,10},{7,3},{... | collective-permute-start | bytes 196616 | tf_op jit(solution)/shard_map/while/body/eval_jaxpr/ppermute | solution.py:17
  214.4 8.2 %collective-permute-start.5 = (f32[1,4,8,1024]{3,2,1,0:T(8,128)S(1)}, f32[1,4,8,1024]{3,2,1,0:T(8,128)S(1)}, u32[]{:S(2)}, u32[]{:S(2)}) collective-permute-start(f32[1,4,8,1024]{3,2,1,0:T(8,128)S(1)} %pad_maximum_fusion.19), channel_id=1, source_target_pairs={{1,0},{2,1},{3,2},{5,4},{6,5},{7,6},{9,8},{10,9},{11,10},{13,12},{... | collective-permute-start | bytes 393224 | tf_op jit(solution)/shard_map/while/body/eval_jaxpr/ppermute | solution.py:25
  223.0 5.2 %collective-permute-start.3 = (f32[1,4,4,1024]{3,2,1,0:T(4,128)S(1)}, f32[1,4,4,1024]{3,2,1,0:T(4,128)S(1)}, u32[]{:S(2)}, u32[]{:S(2)}) collective-permute-start(f32[1,4,4,1024]{3,2,1,0:T(4,128)S(1)} %get-tuple-element.1541), channel_id=1, source_target_pairs={{0,4},{4,8},{8,12},{1,5},{5,9},{9,13},{2,6},{6,10},{10,14},{3,7},{... | collective-permute-start | bytes 196616 | tf_op jit(solution)/shard_map/while/body/eval_jaxpr/ppermute | solution.py:16
  226.3 6.2 %collective-permute-start.4 = (f32[1,4,4,1024]{3,2,1,0:T(4,128)S(1)}, f32[1,4,4,1024]{3,2,1,0:T(4,128)S(1)}, u32[]{:S(2)}, u32[]{:S(2)}) collective-permute-start(f32[1,4,4,1024]{3,2,1,0:T(4,128)S(1)} %get-tuple-element.1542), channel_id=1, source_target_pairs={{4,0},{8,4},{12,8},{5,1},{9,5},{13,9},{6,2},{10,6},{14,10},{7,3},{... | collective-permute-start | bytes 196616 | tf_op jit(solution)/shard_map/while/body/eval_jaxpr/ppermute | solution.py:17
  239.9 4.9 %collective-permute-start.5 = (f32[1,4,8,1024]{3,2,1,0:T(8,128)S(1)}, f32[1,4,8,1024]{3,2,1,0:T(8,128)S(1)}, u32[]{:S(2)}, u32[]{:S(2)}) collective-permute-start(f32[1,4,8,1024]{3,2,1,0:T(8,128)S(1)} %pad_maximum_fusion.19), channel_id=1, source_target_pairs={{1,0},{2,1},{3,2},{5,4},{6,5},{7,6},{9,8},{10,9},{11,10},{13,12},{... | collective-permute-start | bytes 393224 | tf_op jit(solution)/shard_map/while/body/eval_jaxpr/ppermute | solution.py:25
  245.2 4.1 %collective-permute-start.8 = (f32[1,4,4,1024]{3,2,1,0:T(4,128)S(1)}, f32[1,4,4,1024]{3,2,1,0:T(4,128)S(1)}, u32[]{:S(2)}, u32[]{:S(2)}) collective-permute-start(f32[1,4,4,1024]{3,2,1,0:T(4,128)S(1)} %get-tuple-element.852), channel_id=1, source_target_pairs={{0,4},{4,8},{8,12},{1,5},{5,9},{9,13},{2,6},{6,10},{10,14},{3,7},{... | collective-permute-start | bytes 196616 | tf_op jit(solution)/shard_map/ppermute | solution.py:16
  247.6 6.2 %collective-permute-start.9 = (f32[1,4,4,1024]{3,2,1,0:T(4,128)S(1)}, f32[1,4,4,1024]{3,2,1,0:T(4,128)S(1)}, u32[]{:S(2)}, u32[]{:S(2)}) collective-permute-start(f32[1,4,4,1024]{3,2,1,0:T(4,128)S(1)} %get-tuple-element.853), channel_id=1, source_target_pairs={{4,0},{8,4},{12,8},{5,1},{9,5},{13,9},{6,2},{10,6},{14,10},{7,3},{... | collective-permute-start | bytes 196616 | tf_op jit(solution)/shard_map/ppermute | solution.py:17
Sparse Core Ops, SparseCore 0:
  262.0 31.4 all-reduce.10
where the time goes:
time: 303 us; the launch traced here: 302 us
  other arithmetic  111 us (37%)
  waiting for transfers between devices  76.1 us (25%)
  starting transfers between devices  59.4 us (20%)
  blocking collectives  28.5 us (9%)
  between operations  15.1 us (5%)
  local copies, waits for them, and re-layouts  10.2 us (3%)
    sub x8, other arithmetic, rotate(): real_part * cosine - imag_part * sine_part  77.1 us
    ppermute x8, starting transfers between devices, padded_2(): before = lax.ppermute(last, axis, up)  31.5 us
    psum x1, waiting for transfers between devices, broadcast(): return lax.psum(block, axis)  30.9 us
    ppermute x8, waiting for transfers between devices, padded_2(): after = lax.ppermute(leading, axis, down)  20.3 us
    ppermute x6, waiting for transfers between devices, from_behind(): lax.ppermute(value, axis, [(source, source + steps) for source in range(l...  18.7 us
    ppermute x6, starting transfers between devices, from_behind(): lax.ppermute(value, axis, [(source, source + steps) for source in range(l...  17.5 us
    all_gather x1, blocking collectives, local(): piece_traces = lax.all_gather(traces, 'lat', axis=0, tiled=True)  15 us
    add x4, other arithmetic, convolve(): out_imag = out_imag + tap_imag * real_piece + tap_real * imag_piece  14.6 us
  transfers between devices with their start and end apart: 23, of which 22 were waited for; matrix products, arithmetic and copies ran while one was open for 2% of the time, Pallas kernels for 0%

commit v1 on v0

v1 whole, which is shorter than its diff:
```python
import functools
import math

import jax
import jax.numpy as jnp
from jax import lax
from jax.experimental import pallas as pl
from jax.experimental.pallas import tpu as pltpu
from jax.sharding import PartitionSpec as P

MESH = pl.DeviceIdType.MESH
LANES = 128


def sin_cos(x):
    turns = jnp.floor(x * (2.0 / math.pi) + 0.5)
    rest = ((x - turns * 1.5703125) - turns * 4.837512969970703e-4) - turns * 7.549789954891882e-8
    z = rest * rest
    s = rest + rest * z * ((-1.9515295891e-4 * z + 8.3321608736e-3) * z - 1.6666654611e-1)
    c = 1.0 - 0.5 * z + z * z * ((2.443315711809948e-5 * z - 1.388731625493765e-3) * z + 4.166664568298827e-2)
    quarter = turns - 4.0 * jnp.floor(turns * 0.25)
    swap = (quarter == 1.0) | (quarter == 3.0)
    sine = jnp.where(swap, c, s)
    cosine = jnp.where(swap, s, c)
    sine = jnp.where(quarter >= 2.0, -sine, sine)
    cosine = jnp.where((quarter == 1.0) | (quarter == 2.0), -cosine, cosine)
    return sine, cosine


def kernel(
    dims,
    source_ref, traces_ref, tiles_ref, offsets_ref, stencil_ref, freq_ref, slow_ref, refl_ref,
    pic_ref, res_ref,
    taps, S, R, W, part, halo, E, refl_all, media, lines, obs_send, obs_recv, obs,
    pic_send, pic_recv, res_send, res_recv,
    halo_send, halo_recv, med_send, med_recv, obs_ssem, obs_rsem, pic_ssem, pic_rsem, res_ssem, res_rsem,
):
    L, D, F, rows, ntap, nblk = dims
    reach = ntap // 2
    K = D
    cols = 8
    share = rows // D
    lat = lax.axis_index("lat")
    depth = lax.axis_index("depth")
    f = lax.rem(depth, F)
    group = depth - f

    barrier = pltpu.get_barrier_semaphore()
    for j in range(1, L):
        pl.semaphore_signal(barrier, inc=1, device_id={"lat": lax.rem(lat + j, L)}, device_id_type=MESH)
    for j in range(1, D):
        pl.semaphore_signal(barrier, inc=1, device_id={"depth": lax.rem(depth + j, D)}, device_id_type=MESH)

    shape = (rows, cols, LANES)
    sub = lax.broadcasted_iota(jnp.int32, shape, 1)
    lane = lax.broadcasted_iota(jnp.int32, shape, 2)
    line = lax.broadcasted_iota(jnp.int32, shape, 0)
    sign = jnp.where(sub < 4, -1.0, 1.0)

    def turn(v):
        n = v.shape[0]
        return pltpu.roll(v, 4, 1) * sign[:n]

    def own_part(v, way, slot):
        vj = turn(v)

        def body(b, carry):
            acc = jnp.zeros(shape, jnp.float32)
            for i in range(ntap):
                a = i - reach
                r0, r1 = max(0, -a), min(rows, rows - a)
                c = taps[way, 0, b * ntap + i] * v[r0 + a:r1 + a] + taps[way, 1, b * ntap + i] * vj[r0 + a:r1 + a]
                pieces = [acc[r0:r1] + c]
                if r0 > 0:
                    pieces.insert(0, acc[:r0])
                if r1 < rows:
                    pieces.append(acc[r1:])
                acc = pieces[0] if len(pieces) == 1 else jnp.concatenate(pieces, axis=0)
            part[slot, b] = acc
            return carry

        lax.fori_loop(0, ntap, body, 0, unroll=True)

    def finish(h, way, slot):
        before, after = halo[h, 0], halo[h, 1]
        before_j, after_j = turn(before), turn(after)
        total = carry_up = carry_down = None
        for bi in range(ntap):
            b = bi - reach
            acc = part[slot, bi]
            top, low = acc[:reach], acc[reach:]
            for a in range(-reach, 0):
                i = a + reach
                c = taps[way, 0, bi * ntap + i] * before[i:] + taps[way, 1, bi * ntap + i] * before_j[i:]
                n = reach - i
                top = top + c if n == reach else jnp.concatenate([top[:n] + c, top[n:]], axis=0)
            for a in range(1, reach + 1):
                i = a + reach
                c = taps[way, 0, bi * ntap + i] * after[:a] + taps[way, 1, bi * ntap + i] * after_j[:a]
                n = reach - a
                low = low + c if n == 0 else jnp.concatenate([low[:n], low[n:] + c], axis=0)
            acc = jnp.concatenate([top, low], axis=0)
            if b != 0:
                acc = pltpu.roll(acc, (-b) % LANES, 2)
            total = acc if total is None else total + acc
            if b > 0:
                c = jnp.where(lane >= LANES - b, acc, 0.0)
                carry_up = c if carry_up is None else carry_up + c
            if b < 0:
                c = jnp.where(lane < -b, acc, 0.0)
                carry_down = c if carry_down is None else carry_down + c
        moved_up = jnp.where((sub == 3) | (sub == 7), 0.0, pltpu.roll(carry_up, cols - 1, 1))
        moved_down = jnp.where((sub == 0) | (sub == 4), 0.0, pltpu.roll(carry_down, 1, 1))
        return (total - carry_up - carry_down) + (moved_up + moved_down)

    def halo_copies(field, h):
        to_next = pltpu.make_async_remote_copy(
            src_ref=field.at[pl.ds(rows - reach, reach)], dst_ref=halo.at[h, 0],
            send_sem=halo_send.at[h, 0], recv_sem=halo_recv.at[h, 0],
            device_id={"lat": jnp.minimum(lat + 1, L - 1)}, device_id_type=MESH)
        to_prev = pltpu.make_async_remote_copy(
            src_ref=field.at[pl.ds(0, reach)], dst_ref=halo.at[h, 1],
            send_sem=halo_send.at[h, 1], recv_sem=halo_recv.at[h, 1],
            device_id={"lat": jnp.maximum(lat - 1, 0)}, device_id_type=MESH)
        return to_next, to_prev

    pending = []

    def send_halo(field, h):
        to_next, to_prev = halo_copies(field, h)

        @pl.when(lat < L - 1)
        def _():
            to_next.start()

        @pl.when(lat > 0)
        def _():
            to_prev.start()

        pending.append((to_next, to_prev))
        return to_next, to_prev

    def wait_halo(copies):
        to_next, to_prev = copies

        @pl.when(lat > 0)
        def _():
            to_next.wait_recv()

        @pl.when(lat < L - 1)
        def _():
            to_prev.wait_recv()

    for c in range(cols):
        S[0, :, c, :] = source_ref[f, :, c * LANES:(c + 1) * LANES]

    @pl.when(lat == 0)
    def _():
        for h in range(3 * K):
            halo[h, 0] = jnp.zeros((reach, cols, LANES), jnp.float32)

    @pl.when(lat == L - 1)
    def _():
        for h in range(3 * K):
            halo[h, 1] = jnp.zeros((reach, cols, LANES), jnp.float32)

    media[depth, 0] = slow_ref[...]
    media[depth, 1] = refl_ref[...]

    def fill(t, carry):
        b = t // ntap
        i = t % ntap
        for part_index, s in ((0, 1.0), (1, -1.0)):
            ahead = stencil_ref[((f * 2 + part_index) * ntap + i) * ntap + b]
            back = stencil_ref[((f * 2 + part_index) * ntap + (ntap - 1 - i)) * ntap + (ntap - 1 - b)]
            taps[0, part_index, t] = jnp.full((cols, LANES), ahead, jnp.float32)
            taps[1, part_index, t] = jnp.full((cols, LANES), back * s, jnp.float32)
        return carry

    lax.fori_loop(0, ntap * ntap, fill, 0, unroll=9)

    for c in range(cols):
        start = pl.multiple_of(f * (cols * LANES) + c * LANES, LANES)
        lines[:, c, :] = traces_ref[:, pl.ds(start, LANES)]
    for j in range(L):
        tile = lax.rem(lat + j, L)
        acc = jnp.zeros(shape, jnp.float32)
        for q in range(nblk):
            target = (tiles_ref[q] - tile) * rows + offsets_ref[q]
            inside = tiles_ref[q] == tile
            target = jnp.where(inside, target, -1)
            acc = acc + jnp.where(line == target, lines[q][None], 0.0)
        obs_send[j] = acc

    pl.semaphore_wait(barrier, (L - 1) + (D - 1))

    s_copy = send_halo(S.at[0], 0)
    med_copies = []
    for j in range(1, D):
        copy = pltpu.make_async_remote_copy(
            src_ref=media.at[depth], dst_ref=media.at[depth],
            send_sem=med_send.at[j - 1], recv_sem=med_recv.at[j - 1],
            device_id={"depth": lax.rem(depth + j, D)}, device_id_type=MESH)
        copy.start()
        med_copies.append(copy)
    obs_copies = []
    for j in range(1, L):
        copy = pltpu.make_async_remote_copy(
            src_ref=obs_send.at[j], dst_ref=obs_recv.at[j - 1],
            send_sem=obs_ssem.at[j - 1], recv_sem=obs_rsem.at[j - 1],
            device_id={"lat": lax.rem(lat + j, L)}, device_id_type=MESH)
        copy.start()
        obs_copies.append(copy)

    def make_phase(k):
        for r in range(rows):
            for half in range(2):
                E[k, 0, r, half * 4:half * 4 + 4, :] = media[k, 0, r * 4:r * 4 + 4, :]
                refl_all[k, r, half * 4:half * 4 + 4, :] = media[k, 1, r * 4:r * 4 + 4, :]
        sine, cosine = sin_cos(freq_ref[f] * E[k, 0])
        E[k, 0] = cosine
        E[k, 1] = sine

    pic_copies = {}

    def r_stage(k, copies):
        if k == 0:
            total = obs_send[0]
            for j in range(1, L):
                obs_copies[j - 1].wait_recv()
                total = total + obs_recv[j - 1]
            obs[...] = total
            R[0] = jnp.where(sub < 4, total, -total)
        else:
            wait_halo(copies)
            v = finish(K + k - 1, 0, 1)
            v = v * E[k - 1, 0] + turn(v) * E[k - 1, 1]
            if k < K:
                R[k] = v
            prod = S[k] * v
            prod = prod - pltpu.roll(prod, 4, 1)
            for r in range(rows):
                pic_send[k - 1, r * 4:r * 4 + 4, :] = prod[r, 0:4, :]
            level = k - 1
            there = jnp.int32(level)
            mine = (level // F) * F
            slot = lax.rem(f + F - 1 - lax.rem(there, F) + F, F)
            copy = pltpu.make_async_remote_copy(
                src_ref=pic_send.at[level], dst_ref=pic_recv.at[slot],
                send_sem=pic_ssem.at[level], recv_sem=pic_rsem.at[slot],
                device_id={"depth": there}, device_id_type=MESH)

            @pl.when((group == mine) & (depth != level))
            def _():
                copy.start()

            pic_copies[level] = copy
        if k < K:
            copies = send_halo(R.at[k], K + k)
            own_part(R[k], 0, 1)
        return copies

    own_part(S[0], 0, 0)
    for copy in med_copies:
        copy.wait_recv()
    make_phase(0)

    r_copy = None
    r_next = 0
    for k in range(K):
        if k > 0:
            own_part(S[k], 0, 0)
            make_phase(k)
            r_copy = r_stage(r_next, r_copy)
            r_next += 1
        wait_halo(s_copy)
        v = finish(k, 0, 0)
        S[k + 1] = v * E[k, 0] + turn(v) * E[k, 1]
        if k < K - 1:
            s_copy = send_halo(S.at[k + 1], k + 1)

    up = None
    for k in reversed(range(K)):
        w = refl_all[k] * S[k + 1]
        if up is not None:
            w = w + up
        w = w * E[k, 0] - turn(w) * E[k, 1]
        W[k] = w
        w_copy = send_halo(W.at[k], 2 * K + k)
        own_part(w, 1, 0)
        if r_next <= K:
            r_copy = r_stage(r_next, r_copy)
            r_next += 1
        wait_halo(w_copy)
        up = finish(2 * K + k, 1, 0)

    res_send[...] = up - obs[...]
    res_copies = []
    for j in range(1, F):
        there = group + lax.rem(f + j, F)
        copy = pltpu.make_async_remote_copy(
            src_ref=res_send.at[pl.ds(there * share, share)], dst_ref=res_recv.at[f],
            send_sem=res_ssem.at[j - 1], recv_sem=res_rsem.at[j - 1],
            device_id={"depth": there}, device_id_type=MESH)
        copy.start()
        res_copies.append(copy)
    res_recv[f] = res_send[pl.ds(depth * share, share)]

    picture = pic_send[depth]
    for j in range(F - 1):
        pltpu.make_async_remote_copy(
            src_ref=pic_send.at[0], dst_ref=pic_recv.at[j],
            send_sem=pic_ssem.at[0], recv_sem=pic_rsem.at[j],
            device_id={"depth": depth}, device_id_type=MESH).wait_recv()
        picture = picture + pic_recv[j]
    pic_ref[...] = picture

    for copy in med_copies:
        copy.wait_send()
    for copy in obs_copies:
        copy.wait_send()
    for to_next, to_prev in pending:
        @pl.when(lat < L - 1)
        def _():
            to_next.wait_send()

        @pl.when(lat > 0)
        def _():
            to_prev.wait_send()
    for level, copy in pic_copies.items():
        @pl.when((group == (level // F) * F) & (depth != level))
        def _():
            copy.wait_send()

    for copy in res_copies:
        copy.wait_recv()
    for g in range(F):
        for r in range(share):
            v = res_recv[g, r]
            for c in range(cols):
                res_ref[r, g:g + 1, c * LANES:(c + 1) * LANES] = v[c:c + 1, :]
    for copy in res_copies:
        copy.wait_send()


def solution(mesh):
    L, D = mesh.shape["lat"], mesh.shape["depth"]

    def local(source, traces, trace_tiles, trace_offsets, stencil, angular_freq, slowness, reflect):
        F, rows, width = source.shape
        nblk = traces.shape[0]
        ntap = stencil.shape[-1]
        cells = slowness.shape[1]
        mrows = cells // LANES
        cols = width // LANES
        share = rows // D
        K = D
        dims = (L, D, F, rows, ntap, nblk)
        reach = ntap // 2
        field = (rows, cols, LANES)
        f32 = jnp.float32
        vmem = pl.BlockSpec(memory_space=pltpu.VMEM)
        smem = pl.BlockSpec(memory_space=pltpu.SMEM)
        picture, residual = pl.pallas_call(
            functools.partial(kernel, dims),
            out_shape=(
                jax.ShapeDtypeStruct((mrows, LANES), f32),
                jax.ShapeDtypeStruct((share, F, width), f32),
            ),
            in_specs=[vmem, vmem, smem, smem, smem, smem, vmem, vmem],
            out_specs=(vmem, vmem),
            scratch_shapes=[
                pltpu.VMEM((2, 2, ntap * ntap, cols, LANES), f32),
                pltpu.VMEM((K + 1,) + field, f32),
                pltpu.VMEM((K,) + field, f32),
                pltpu.VMEM((K,) + field, f32),
                pltpu.VMEM((2, ntap) + field, f32),
                pltpu.VMEM((3 * K, 2, reach, cols, LANES), f32),
                pltpu.VMEM((K, 2) + field, f32),
                pltpu.VMEM((K,) + field, f32),
                pltpu.VMEM((D, 2, mrows, LANES), f32),
                pltpu.VMEM((nblk, cols, LANES), f32),
                pltpu.VMEM((L,) + field, f32),
                pltpu.VMEM((L - 1,) + field, f32),
                pltpu.VMEM(field, f32),
                pltpu.VMEM((K, mrows, LANES), f32),
                pltpu.VMEM((F, mrows, LANES), f32),
                pltpu.VMEM(field, f32),
                pltpu.VMEM((F, share, cols, LANES), f32),
                pltpu.SemaphoreType.DMA((3 * K, 2)),
                pltpu.SemaphoreType.DMA((3 * K, 2)),
                pltpu.SemaphoreType.DMA((D - 1,)),
                pltpu.SemaphoreType.DMA((D - 1,)),
                pltpu.SemaphoreType.DMA((L - 1,)),
                pltpu.SemaphoreType.DMA((L - 1,)),
                pltpu.SemaphoreType.DMA((K,)),
                pltpu.SemaphoreType.DMA((F,)),
                pltpu.SemaphoreType.DMA((F - 1,)),
                pltpu.SemaphoreType.DMA((F - 1,)),
            ],
            compiler_params=pltpu.CompilerParams(
                collective_id=0, has_side_effects=True, vmem_limit_bytes=32 * 1024 * 1024
            ),
        )(
            source, traces, trace_tiles.reshape(-1), trace_offsets, stencil.reshape(-1), angular_freq,
            slowness.reshape(mrows, LANES), reflect.reshape(mrows, LANES),
        )
        return picture.reshape(1, cells), residual

    in_specs = (
        P("shots", "lat", None),
        P(("shots", "lat"), None),
        P(("shots", "lat"), None),
        P(("shots", "lat")),
        P(),
        P(),
        P("depth", "lat"),
        P("depth", "lat"),
    )
    out_specs = (P(("shots", "depth"), "lat"), P(("shots", "lat", "depth"), None, None))
    return jax.shard_map(local, mesh=mesh, in_specs=in_specs, out_specs=out_specs, check_vma=False)
```

time: 303 us -> 37.4 us (0.12)
  other arithmetic: 111 us -> 0 us
  waiting for transfers between devices: 76.1 us -> 0 us
  starting transfers between devices: 59.4 us -> 0 us
  Pallas kernels: 0 us -> 32.8 us
  blocking collectives: 28.5 us -> 0 us
  between operations: 15.1 us -> 0.7 us
  local copies, waits for them, and re-layouts: 10.2 us -> 3.64 us
    sub x14 -> x0, other arithmetic: 92.6 us -> none  [the longest x8 77.1 us: rotate(): real_part * cosine - imag_part * sine_part]
    ppermute x22 -> x0, starting transfers between devices: 59.4 us -> none  [the longest x8 31.5 us: padded_2(): before = lax.ppermute(last, axis, up)]
    ppermute x22 -> x0, waiting for transfers between devices: 45.1 us -> none  [the longest x8 20.3 us: padded_2(): after = lax.ppermute(leading, axis, down)]
    pallas_call x0 -> x1, Pallas kernels: none -> 32.8 us  [local(): pl.pallas_call(functools.partial(kernel, dims), out_shape=(jax.ShapeDtype...]
    psum x1 -> x0, waiting for transfers between devices: 30.9 us -> none  [broadcast(): return lax.psum(block, axis)]
    all_gather x1 -> x0, blocking collectives: 15 us -> none  [local(): piece_traces = lax.all_gather(traces, 'lat', axis=0, tiled=True)]
    add x15 -> x0, other arithmetic: 14.9 us -> none  [the longest x4 14.6 us: convolve(): out_imag = out_imag + tap_imag * real_piece + tap_real * imag_piece]
    unnamed x1 -> x0, blocking collectives: 13.5 us -> none
  transfers between devices with their start and end apart: 23 -> 0, of which waited for: 22 -> 0; matrix products, arithmetic and copies ran while one was open for 2% -> 0% of each run, Pallas kernels for 0% -> 0%
where the time goes in v1:
time: 37.4 us; the launch traced here: 37.1 us
  Pallas kernels  32.8 us (88%)
  local copies, waits for them, and re-layouts  3.64 us (10%)
  between operations  0.7 us (2%)
    pallas_call x1, Pallas kernels, local(): pl.pallas_call(functools.partial(kernel, dims), out_shape=(jax.ShapeDtype...  32.8 us
    unnamed x17, local copies, waits for them, and re-layouts  3.51 us

profile of v1, /device:TPU:0, one launch (start us, length us, event | category | flops | bytes accessed | tf_op | source)
XLA Modules:
  0.0 37.1 jit_solution(10922952229252591917)
XLA Ops:
  0.6 0.0 copy-start
  0.6 0.8 %copy.10 = f32[4,2,9,9]{3,2,1,0:T(8,128)S(1)} copy(f32[4,2,9,9]{3,1,2,0:T(2,128)} %param.12) | data formatting | bytes 5184 | tf_op args[4]
  1.5 0.0 copy-start.2
  1.5 0.0 copy-start.3
  1.5 0.0 copy-start.4
  1.5 0.0 copy-start.5
  1.5 0.0 copy-start.6
  1.5 0.1 reshape.20.stencil_ref
  1.7 0.0 copy-done
  1.7 0.5 %copy-done.2 = f32[1,4096]{1,0:T(1,128)S(1)} copy-done((f32[1,4096]{1,0:T(1,128)S(1)}, f32[1,4096]{1,0:T(1,128)}, u32[]{:S(2)}) %copy-start.2) | copy-done | bytes 16408
  2.2 0.0 copy-done.3
  2.2 0.0 copy-done.4
  2.2 0.0 copy-done.5
  2.2 0.0 copy-done.6
  2.2 0.0 copy-start.1
  2.2 0.9 %copy-done.1 = f32[8,4096]{1,0:T(8,128)S(1)} copy-done((f32[8,4096]{1,0:T(8,128)S(1)}, f32[8,4096]{1,0:T(8,128)}, u32[]{:S(2)}) %copy-start.1) | copy-done | bytes 131096
  3.1 32.8 %shard_map.95 = (f32[32,128]{1,0:T(8,128)S(1)}, f32[2,4,1024]{2,1,0:T(4,128)S(1)}) custom-call(f32[4,8,1024]{2,1,0:T(8,128)S(1)} %copy-done, f32[8,4096]{1,0:T(8,128)S(1)} %copy-done.1, s32[8]{0:T(128)S(1)} %bitcast.7, s32[8]{0:T(128)S(1)} %copy-done.5, f32[648]{0:T(1024)S(1)} %reshape.20.stencil_ref, f32[4]{0:T(128)S(1)} %copy-done.6, ...), custom_call_target="tpu_custom_call" | custom-call | tf_op jit(solution)/shard_map/pallas_call | solution.py:364
  35.9 0.6 %copy.13 = f32[1,4096]{1,0:T(1,128)} copy(f32[1,4096]{1,0:T(1,128)S(1)} %bitcast.6) | data formatting | bytes 32768
  36.5 0.6 %copy.14 = f32[2,4,1024]{2,1,0:T(4,128)} copy(f32[2,4,1024]{2,1,0:T(4,128)S(1)} %get-tuple-element.9) | data formatting | bytes 65536
Async XLA Ops:
  0.6 1.0 %copy-start = (f32[4,8,1024]{2,1,0:T(8,128)S(1)}, f32[4,8,1024]{2,1,0:T(8,128)}, u32[]{:S(2)}) copy-start(f32[4,8,1024]{2,1,0:T(8,128)} %source_ref.1) | copy-start | bytes 393220
  1.5 0.7 %copy-start.2 = (f32[1,4096]{1,0:T(1,128)S(1)}, f32[1,4096]{1,0:T(1,128)}, u32[]{:S(2)}) copy-start(f32[1,4096]{1,0:T(1,128)} %param.14) | copy-start | bytes 49156
  1.5 0.7 %copy-start.3 = (f32[1,4096]{1,0:T(1,128)S(1)}, f32[1,4096]{1,0:T(1,128)}, u32[]{:S(2)}) copy-start(f32[1,4096]{1,0:T(1,128)} %param.15) | copy-start | bytes 49156
  1.5 0.7 %copy-start.4 = (s32[8,1]{0,1:T(1,128)S(1)}, s32[8,1]{0,1:T(1,128)}, u32[]{:S(2)}) copy-start(s32[8,1]{0,1:T(1,128)} %param.10) | copy-start | bytes 100
  1.5 0.7 %copy-start.5 = (s32[8]{0:T(128)S(1)}, s32[8]{0:T(128)}, u32[]{:S(2)}) copy-start(s32[8]{0:T(128)} %offsets_ref.1) | copy-start | bytes 100
  1.5 0.7 %copy-start.6 = (f32[4]{0:T(128)S(1)}, f32[4]{0:T(128)}, u32[]{:S(2)}) copy-start(f32[4]{0:T(128)} %freq_ref.1) | copy-start | bytes 52
  2.2 0.9 %copy-start.1 = (f32[8,4096]{1,0:T(8,128)S(1)}, f32[8,4096]{1,0:T(8,128)}, u32[]{:S(2)}) copy-start(f32[8,4096]{1,0:T(8,128)} %traces_ref.1) | copy-start | bytes 393220

commit v2 on v1

v2 whole, which is shorter than its diff:
```python
import functools
import math

import jax
import jax.numpy as jnp
from jax import lax
from jax.experimental import pallas as pl
from jax.experimental.pallas import tpu as pltpu
from jax.sharding import PartitionSpec as P

MESH = pl.DeviceIdType.MESH
LANES = 128


def sin_cos(x):
    turns = jnp.floor(x * (2.0 / math.pi) + 0.5)
    rest = ((x - turns * 1.5703125) - turns * 4.837512969970703e-4) - turns * 7.549789954891882e-8
    z = rest * rest
    s = rest + rest * z * ((-1.9515295891e-4 * z + 8.3321608736e-3) * z - 1.6666654611e-1)
    c = 1.0 - 0.5 * z + z * z * ((2.443315711809948e-5 * z - 1.388731625493765e-3) * z + 4.166664568298827e-2)
    quarter = turns - 4.0 * jnp.floor(turns * 0.25)
    swap = (quarter == 1.0) | (quarter == 3.0)
    sine = jnp.where(swap, c, s)
    cosine = jnp.where(swap, s, c)
    sine = jnp.where(quarter >= 2.0, -sine, sine)
    cosine = jnp.where((quarter == 1.0) | (quarter == 2.0), -cosine, cosine)
    return sine, cosine


def kernel(
    dims,
    source_ref, traces_ref, tiles_ref, offsets_ref, stencil_ref, freq_ref, slow_ref, refl_ref,
    pic_ref, res_ref,
    taps, S, R, W, part, halo, E, refl_all, media, media_edge, lines, obs_send, obs_recv, obs,
    pic_send, pic_recv, res_send, res_recv,
    halo_send, halo_recv, med_send, med_recv, edge_send, edge_recv, obs_ssem, obs_rsem, pic_ssem, pic_rsem, res_ssem, res_rsem,
):
    L, D, F, rows, ntap, nblk = dims
    reach = ntap // 2
    K = D
    cols = 8
    share = rows // D
    lat = lax.axis_index("lat")
    depth = lax.axis_index("depth")
    f = lax.rem(depth, F)
    group = depth - f

    barrier = pltpu.get_barrier_semaphore()
    for j in range(1, L):
        pl.semaphore_signal(barrier, inc=1, device_id={"lat": lax.rem(lat + j, L)}, device_id_type=MESH)
    for j in range(1, D):
        there = lax.rem(depth + j, D)
        pl.semaphore_signal(barrier, inc=1, device_id={"depth": there}, device_id_type=MESH)
        for side in (1, L - 1):
            pl.semaphore_signal(
                barrier, inc=1, device_id={"lat": lax.rem(lat + side, L), "depth": there}, device_id_type=MESH)

    shape = (rows, cols, LANES)
    sub = lax.broadcasted_iota(jnp.int32, shape, 1)
    lane = lax.broadcasted_iota(jnp.int32, shape, 2)
    line = lax.broadcasted_iota(jnp.int32, shape, 0)
    sign = jnp.where(sub < 4, -1.0, 1.0)[:1]
    own = slice(reach, reach + rows)
    wide = rows + 2 * reach

    def turn(v):
        return pltpu.roll(v, 4, 1) * sign

    def rotate(v, k, lines_of, way):
        return v * E[k, 0, lines_of] + way * (turn(v) * E[k, 1, lines_of])

    def add_lines(acc, c, first):
        last = first + c.shape[0]
        pieces = [acc[first:last] + c]
        if first > 0:
            pieces.insert(0, acc[:first])
        if last < acc.shape[0]:
            pieces.append(acc[last:])
        return pieces[0] if len(pieces) == 1 else jnp.concatenate(pieces, axis=0)

    def tap(way, bi, a, v, vj):
        t = bi * ntap + a + reach
        return taps[way, 0, t] * v + taps[way, 1, t] * vj

    def own_part(v, way, slot):
        vj = turn(v)

        def body(b, carry):
            acc = jnp.zeros((wide, cols, LANES), jnp.float32)
            for a in range(-reach, reach + 1):
                acc = add_lines(acc, tap(way, b, a, v, vj), reach - a)
            part[slot, b] = acc
            return carry

        lax.fori_loop(0, ntap, body, 0, unroll=True)

    def shifted_sum(terms):
        total = carry_up = carry_down = None
        for bi in range(ntap):
            b = bi - reach
            acc = terms(bi)
            if b != 0:
                acc = pltpu.roll(acc, (-b) % LANES, 2)
            total = acc if total is None else total + acc
            if b > 0:
                c = jnp.where(lane >= LANES - b, acc, 0.0)
                carry_up = c if carry_up is None else carry_up + c
            if b < 0:
                c = jnp.where(lane < -b, acc, 0.0)
                carry_down = c if carry_down is None else carry_down + c
        moved_up = jnp.where((sub == 3) | (sub == 7), 0.0, pltpu.roll(carry_up, cols - 1, 1))
        moved_down = jnp.where((sub == 0) | (sub == 4), 0.0, pltpu.roll(carry_down, 1, 1))
        return (total - carry_up - carry_down) + (moved_up + moved_down)

    def finish(h, way, slot):
        before, after = halo[h, 0], halo[h, 1]
        before_j, after_j = turn(before), turn(after)

        def low(bi):
            acc = part[slot, bi, :rows]
            for a in range(-reach, reach):
                acc = add_lines(acc, tap(way, bi, a, before[reach + a:], before_j[reach + a:]), 0)
            return acc

        def high(bi):
            acc = part[slot, bi, rows:]
            for a in range(1 - reach, reach + 1):
                acc = add_lines(acc, tap(way, bi, a, after[:reach + a], after_j[:reach + a]), reach - a)
            return acc

        return jnp.concatenate([shifted_sum(low), shifted_sum(high)], axis=0)

    def narrow(v, way):
        vj = turn(v)

        def terms(bi):
            acc = tap(way, bi, -reach, v[:rows], vj[:rows])
            for i in range(1, ntap):
                acc = acc + tap(way, bi, i - reach, v[i:i + rows], vj[i:i + rows])
            return acc

        return shifted_sum(terms)

    def halo_copies(field, h):
        to_next = pltpu.make_async_remote_copy(
            src_ref=field, dst_ref=halo.at[h, 0],
            send_sem=halo_send.at[h, 0], recv_sem=halo_recv.at[h, 0],
            device_id={"lat": jnp.minimum(lat + 1, L - 1)}, device_id_type=MESH)
        to_prev = pltpu.make_async_remote_copy(
            src_ref=field, dst_ref=halo.at[h, 1],
            send_sem=halo_send.at[h, 1], recv_sem=halo_recv.at[h, 1],
            device_id={"lat": jnp.maximum(lat - 1, 0)}, device_id_type=MESH)
        return to_next, to_prev

    pending = []

    def send_halo(field, h):
        to_next, to_prev = halo_copies(field, h)

        @pl.when(lat < L - 1)
        def _():
            to_next.start()

        @pl.when(lat > 0)
        def _():
            to_prev.start()

        pending.append((to_next, to_prev))
        return to_next, to_prev

    def wait_halo(copies):
        to_next, to_prev = copies

        @pl.when(lat > 0)
        def _():
            to_next.wait_recv()

        @pl.when(lat < L - 1)
        def _():
            to_prev.wait_recv()

    for c in range(cols):
        S[0, own, c, :] = source_ref[f, :, c * LANES:(c + 1) * LANES]

    blocks = K // 2
    for side, edge in ((0, lat == 0), (1, lat == L - 1)):
        @pl.when(edge)
        def _():
            for h in range(3 * blocks):
                halo[h, side] = jnp.zeros(shape, jnp.float32)
            for b in range(blocks):
                media_edge[b, side] = jnp.zeros(media_edge.shape[2:], jnp.float32)

    media[depth, 0] = slow_ref[...]
    media[depth, 1] = refl_ref[...]

    def fill(t, carry):
        b = t // ntap
        i = t % ntap
        for part_index, s in ((0, 1.0), (1, -1.0)):
            ahead = stencil_ref[f, i, part_index, b]
            back = stencil_ref[f, ntap - 1 - i, part_index, ntap - 1 - b]
            taps[0, part_index, t] = jnp.full((cols, LANES), ahead, jnp.float32)
            taps[1, part_index, t] = jnp.full((cols, LANES), back * s, jnp.float32)
        return carry

    lax.fori_loop(0, ntap * ntap, fill, 0, unroll=9)

    for c in range(cols):
        start = pl.multiple_of(f * (cols * LANES) + c * LANES, LANES)
        lines[:, c, :] = traces_ref[:, pl.ds(start, LANES)]
    for j in range(L):
        tile = lax.rem(lat + j, L)
        acc = jnp.zeros(shape, jnp.float32)
        for q in range(nblk):
            target = (tiles_ref[q] - tile) * rows + offsets_ref[q]
            inside = tiles_ref[q] == tile
            target = jnp.where(inside, target, -1)
            acc = acc + jnp.where(line == target, lines[q][None], 0.0)
        obs_send[j] = acc

    own_part(S[0, own], 0, 0)

    pl.semaphore_wait(barrier, (L - 1) + 3 * (D - 1))

    s_copy = send_halo(S.at[0, pl.ds(reach, rows)], 0)
    med_copies = []
    for j in range(1, D):
        copy = pltpu.make_async_remote_copy(
            src_ref=media.at[depth], dst_ref=media.at[depth],
            send_sem=med_send.at[j - 1], recv_sem=med_recv.at[j - 1],
            device_id={"depth": lax.rem(depth + j, D)}, device_id_type=MESH)
        copy.start()
        med_copies.append(copy)
    edge_rows = media.shape[2] // 2
    edge_copies = []
    even = lax.rem(depth, 2) == 0
    for side in range(2):
        place = jnp.minimum(lat + 1, L - 1) if side == 0 else jnp.maximum(lat - 1, 0)
        has = lat < L - 1 if side == 0 else lat > 0
        for j in range(D):
            copy = pltpu.make_async_remote_copy(
                src_ref=media.at[depth, :, pl.ds((1 - side) * edge_rows, edge_rows)],
                dst_ref=media_edge.at[depth // 2, side],
                send_sem=edge_send.at[side, j], recv_sem=edge_recv.at[side, depth // 2],
                device_id={"lat": place, "depth": lax.rem(depth + j, D)}, device_id_type=MESH)

            @pl.when(has & even)
            def _():
                copy.start()

            edge_copies.append((has & even, copy))

    def wait_edges():
        for side in range(2):
            for b in range(blocks):
                @pl.when(lat > 0 if side == 0 else lat < L - 1)
                def _():
                    pltpu.make_async_remote_copy(
                        src_ref=media.at[depth, :, pl.ds((1 - side) * edge_rows, edge_rows)],
                        dst_ref=media_edge.at[b, side],
                        send_sem=edge_send.at[side, 0], recv_sem=edge_recv.at[side, b],
                        device_id={"depth": depth}, device_id_type=MESH).wait_recv()

    obs_copies = []
    for j in range(1, L):
        copy = pltpu.make_async_remote_copy(
            src_ref=obs_send.at[j], dst_ref=obs_recv.at[j - 1],
            send_sem=obs_ssem.at[j - 1], recv_sem=obs_rsem.at[j - 1],
            device_id={"lat": lax.rem(lat + j, L)}, device_id_type=MESH)
        copy.start()
        obs_copies.append(copy)

    inside_low = jnp.where(lat > 0, 1.0, 0.0)
    inside_high = jnp.where(lat < L - 1, 1.0, 0.0)

    def make_phase(k):
        for half in range(2):
            subs = slice(half * 4, half * 4 + 4)
            for r in range(rows):
                E[k, 0, reach + r, subs, :] = media[k, 0, r * 4:r * 4 + 4, :]
                refl_all[k, reach + r, subs, :] = media[k, 1, r * 4:r * 4 + 4, :]
            if k % 2 == 0:
                for side in range(2):
                    for r in range(reach):
                        at = side * (reach + rows) + r
                        E[k, 0, at, subs, :] = media_edge[k // 2, side, 0, r * 4:r * 4 + 4, :]
                        refl_all[k, at, subs, :] = media_edge[k // 2, side, 1, r * 4:r * 4 + 4, :]
        pieces = [(own, None)]
        if k % 2 == 0:
            pieces += [(slice(0, reach), inside_low), (slice(reach + rows, wide), inside_high)]
        for where, scale in pieces:
            sine, cosine = sin_cos(freq_ref[f] * E[k, 0, where])
            E[k, 0, where] = cosine if scale is None else cosine * scale
            E[k, 1, where] = sine if scale is None else sine * scale

    pic_copies = {}

    def send_picture(level, v):
        prod = S[level + 1, own] * v
        prod = prod - pltpu.roll(prod, 4, 1)
        for r in range(rows):
            pic_send[level, r * 4:r * 4 + 4, :] = prod[r, 0:4, :]
        there = jnp.int32(level)
        slot = lax.rem(f + F - 1 - lax.rem(there, F) + F, F)
        copy = pltpu.make_async_remote_copy(
            src_ref=pic_send.at[level], dst_ref=pic_recv.at[slot],
            send_sem=pic_ssem.at[level], recv_sem=pic_rsem.at[slot],
            device_id={"depth": there}, device_id_type=MESH)

        @pl.when((group == (level // F) * F) & (depth != level))
        def _():
            copy.start()

        pic_copies[level] = copy

    def r_stage(b, copies):
        if b == 0:
            total = obs_send[0]
            for j in range(1, L):
                obs_copies[j - 1].wait_recv()
                total = total + obs_recv[j - 1]
            obs[...] = total
            R[0] = jnp.where(sub < 4, total, -total)
        else:
            k = 2 * b - 2
            wait_halo(copies)
            v = rotate(finish(blocks + b - 1, 0, 1), k, slice(0, wide), 1.0)
            send_picture(k, v[own])
            v = rotate(narrow(v, 0), k + 1, own, 1.0)
            if b < blocks:
                R[b] = v
        if b < blocks:
            copies = send_halo(R.at[b], blocks + b)
            own_part(R[b], 0, 1)
        if b > 0:
            send_picture(k + 1, v)
        return copies

    r_copy = None
    r_next = 0
    for b in range(blocks):
        k = 2 * b
        if b > 0:
            own_part(S[k, own], 0, 0)
            make_phase(k)
            make_phase(k + 1)
            r_copy = r_stage(r_next, r_copy)
            r_next += 1
        wait_halo(s_copy)
        v = finish(b, 0, 0)
        if b == 0:
            for copy in med_copies:
                copy.wait_recv()
            wait_edges()
            make_phase(0)
            make_phase(1)
        v = rotate(v, k, slice(0, wide), 1.0)
        S[k + 1] = v
        v = rotate(narrow(v, 0), k + 1, own, 1.0)
        S[k + 2, own] = v
        if b < blocks - 1:
            s_copy = send_halo(S.at[k + 2, pl.ds(reach, rows)], b + 1)

    up = None
    for b in reversed(range(blocks)):
        k = 2 * b
        w = refl_all[k + 1, own] * S[k + 2, own]
        if up is not None:
            w = w + up
        w = rotate(w, k + 1, own, -1.0)
        W[b] = w
        w_copy = send_halo(W.at[b], 2 * blocks + b)
        own_part(w, 1, 0)
        if r_next <= blocks:
            r_copy = r_stage(r_next, r_copy)
            r_next += 1
        wait_halo(w_copy)
        w = finish(2 * blocks + b, 1, 0) + refl_all[k] * S[k + 1]
        up = narrow(rotate(w, k, slice(0, wide), -1.0), 1)

    res_send[...] = up - obs[...]
    res_copies = []
    for j in range(1, F):
        there = group + lax.rem(f + j, F)
        copy = pltpu.make_async_remote_copy(
            src_ref=res_send.at[pl.ds(there * share, share)], dst_ref=res_recv.at[f],
            send_sem=res_ssem.at[j - 1], recv_sem=res_rsem.at[j - 1],
            device_id={"depth": there}, device_id_type=MESH)
        copy.start()
        res_copies.append(copy)
    res_recv[f] = res_send[pl.ds(depth * share, share)]

    picture = pic_send[depth]
    for j in range(F - 1):
        pltpu.make_async_remote_copy(
            src_ref=pic_send.at[0], dst_ref=pic_recv.at[j],
            send_sem=pic_ssem.at[0], recv_sem=pic_rsem.at[j],
            device_id={"depth": depth}, device_id_type=MESH).wait_recv()
        picture = picture + pic_recv[j]
    pic_ref[...] = picture

    for copy in med_copies:
        copy.wait_send()
    for copy in obs_copies:
        copy.wait_send()
    for started, copy in edge_copies:
        @pl.when(started)
        def _():
            copy.wait_send()
    for to_next, to_prev in pending:
        @pl.when(lat < L - 1)
        def _():
            to_next.wait_send()

        @pl.when(lat > 0)
        def _():
            to_prev.wait_send()
    for level, copy in pic_copies.items():
        @pl.when((group == (level // F) * F) & (depth != level))
        def _():
            copy.wait_send()

    for copy in res_copies:
        copy.wait_recv()
    for g in range(F):
        for r in range(share):
            v = res_recv[g, r]
            for c in range(cols):
                res_ref[r, g:g + 1, c * LANES:(c + 1) * LANES] = v[c:c + 1, :]
    for copy in res_copies:
        copy.wait_send()


def solution(mesh):
    L, D = mesh.shape["lat"], mesh.shape["depth"]

    def local(source, traces, trace_tiles, trace_offsets, stencil, angular_freq, slowness, reflect):
        F, rows, width = source.shape
        nblk = traces.shape[0]
        ntap = stencil.shape[-1]
        cells = slowness.shape[1]
        mrows = cells // LANES
        cols = width // LANES
        share = rows // D
        K = D
        dims = (L, D, F, rows, ntap, nblk)
        reach = ntap // 2
        field = (rows, cols, LANES)
        broad = (rows + 2 * reach, cols, LANES)
        blocks = K // 2
        f32 = jnp.float32
        vmem = pl.BlockSpec(memory_space=pltpu.VMEM)
        smem = pl.BlockSpec(memory_space=pltpu.SMEM)
        picture, residual = pl.pallas_call(
            functools.partial(kernel, dims),
            out_shape=(
                jax.ShapeDtypeStruct((mrows, LANES), f32),
                jax.ShapeDtypeStruct((share, F, width), f32),
            ),
            in_specs=[vmem, vmem, smem, smem, smem, smem, vmem, vmem],
            out_specs=(vmem, vmem),
            scratch_shapes=[
                pltpu.VMEM((2, 2, ntap * ntap, cols, LANES), f32),
                pltpu.VMEM((K + 1,) + broad, f32),
                pltpu.VMEM((blocks,) + field, f32),
                pltpu.VMEM((blocks,) + field, f32),
                pltpu.VMEM((2, ntap) + broad, f32),
                pltpu.VMEM((3 * blocks, 2) + field, f32),
                pltpu.VMEM((K, 2) + broad, f32),
                pltpu.VMEM((K,) + broad, f32),
                pltpu.VMEM((D, 2, mrows, LANES), f32),
                pltpu.VMEM((blocks, 2, 2, mrows // 2, LANES), f32),
                pltpu.VMEM((nblk, cols, LANES), f32),
                pltpu.VMEM((L,) + field, f32),
                pltpu.VMEM((L - 1,) + field, f32),
                pltpu.VMEM(field, f32),
                pltpu.VMEM((K, mrows, LANES), f32),
                pltpu.VMEM((F, mrows, LANES), f32),
                pltpu.VMEM(field, f32),
                pltpu.VMEM((F, share, cols, LANES), f32),
                pltpu.SemaphoreType.DMA((3 * blocks, 2)),
                pltpu.SemaphoreType.DMA((3 * blocks, 2)),
                pltpu.SemaphoreType.DMA((D - 1,)),
                pltpu.SemaphoreType.DMA((D - 1,)),
                pltpu.SemaphoreType.DMA((2, D)),
                pltpu.SemaphoreType.DMA((2, blocks)),
                pltpu.SemaphoreType.DMA((L - 1,)),
                pltpu.SemaphoreType.DMA((L - 1,)),
                pltpu.SemaphoreType.DMA((K,)),
                pltpu.SemaphoreType.DMA((F,)),
                pltpu.SemaphoreType.DMA((F - 1,)),
                pltpu.SemaphoreType.DMA((F - 1,)),
            ],
            compiler_params=pltpu.CompilerParams(
                collective_id=0, has_side_effects=True, vmem_limit_bytes=32 * 1024 * 1024
            ),
        )(
            source, traces, trace_tiles.reshape(-1), trace_offsets, stencil.transpose(0, 2, 1, 3), angular_freq,
            slowness.reshape(mrows, LANES), reflect.reshape(mrows, LANES),
        )
        return picture.reshape(1, cells), residual

    in_specs = (
        P("shots", "lat", None),
        P(("shots", "lat"), None),
        P(("shots", "lat"), None),
        P(("shots", "lat")),
        P(),
        P(),
        P("depth", "lat"),
        P("depth", "lat"),
    )
    out_specs = (P(("shots", "depth"), "lat"), P(("shots", "lat", "depth"), None, None))
    return jax.shard_map(local, mesh=mesh, in_specs=in_specs, out_specs=out_specs, check_vma=False)
```

time: 37.4 us -> 34.2 us (0.914)
  Pallas kernels: 32.8 us -> 27.3 us
  local copies, waits for them, and re-layouts: 3.64 us -> 5.89 us
    pallas_call x1, Pallas kernels: 32.8 us -> 27.3 us  [local(): pl.pallas_call(functools.partial(kernel, dims), out_shape=(jax.ShapeDtype...]
    unnamed x17 -> x18, local copies, waits for them, and re-layouts: 3.51 us -> 5.89 us
where the time goes in v2:
time: 34.2 us; the launch traced here: 33.9 us
  Pallas kernels  27.3 us (80%)
  local copies, waits for them, and re-layouts  5.89 us (17%)
  between operations  0.67 us (2%)
    pallas_call x1, Pallas kernels, local(): pl.pallas_call(functools.partial(kernel, dims), out_shape=(jax.ShapeDtype...  27.3 us
    unnamed x18, local copies, waits for them, and re-layouts  5.89 us

profile of v2, /device:TPU:0, one launch (start us, length us, event | category | flops | bytes accessed | tf_op | source)
XLA Modules:
  0.0 33.9 jit_solution(16961826904933525053)
XLA Ops:
  0.6 0.0 copy-start.5
  0.6 0.0 copy-start.6
  0.7 0.0 copy-start.7
  0.7 0.6 %copy-done.5 = s32[8,1]{0,1:T(1,128)S(1)} copy-done((s32[8,1]{0,1:T(1,128)S(1)}, s32[8,1]{0,1:T(1,128)}, u32[]{:S(2)}) %copy-start.5) | copy-done | bytes 56
  1.3 0.0 copy-done.6
  1.3 0.0 copy-done.7
  1.3 0.0 copy-start
  1.3 0.9 %copy-done = f32[4,8,1024]{2,1,0:T(8,128)S(1)} copy-done((f32[4,8,1024]{2,1,0:T(8,128)S(1)}, f32[4,8,1024]{2,1,0:T(8,128)}, u32[]{:S(2)}) %copy-start) | copy-done | bytes 131096
  2.2 0.0 copy-start.1
  2.2 0.9 %copy-done.1 = f32[8,4096]{1,0:T(8,128)S(1)} copy-done((f32[8,4096]{1,0:T(8,128)S(1)}, f32[8,4096]{1,0:T(8,128)}, u32[]{:S(2)}) %copy-start.1) | copy-done | bytes 131096
  3.1 0.0 copy-start.2
  3.1 0.8 %copy-done.2 = f32[4,2,9,9]{3,1,2,0:T(2,128)S(1)} copy-done((f32[4,2,9,9]{3,1,2,0:T(2,128)S(1)}, f32[4,2,9,9]{3,1,2,0:T(2,128)}, u32[]{:S(2)}) %copy-start.2) | copy-done | bytes 2616
  3.9 0.0 copy-start.3
  3.9 0.7 %copy-done.3 = f32[1,4096]{1,0:T(1,128)S(1)} copy-done((f32[1,4096]{1,0:T(1,128)S(1)}, f32[1,4096]{1,0:T(1,128)}, u32[]{:S(2)}) %copy-start.3) | copy-done | bytes 16408
  4.6 0.0 copy-start.4
  4.6 0.7 %copy-done.4 = f32[1,4096]{1,0:T(1,128)S(1)} copy-done((f32[1,4096]{1,0:T(1,128)S(1)}, f32[1,4096]{1,0:T(1,128)}, u32[]{:S(2)}) %copy-start.4) | copy-done | bytes 16408
  5.3 27.3 %shard_map.95 = (f32[32,128]{1,0:T(8,128)S(1)}, f32[2,4,1024]{2,1,0:T(4,128)S(1)}) custom-call(f32[4,8,1024]{2,1,0:T(8,128)S(1)} %copy-done, f32[8,4096]{1,0:T(8,128)S(1)} %copy-done.1, s32[8]{0:T(128)S(1)} %bitcast.9, s32[8]{0:T(128)S(1)} %copy-done.6, f32[4,9,2,9]{3,2,1,0:T(2,128)S(1)} %bitcast.5, f32[4]{0:T(128)S(1)} %copy-done.7, f32[32,128]{1,0:T(8,128)S(1)} %bitcast.7, ...), custom_call_target="tpu_custom_call" | custom-call | tf_op jit(solution)/shard_map/pallas_call | solution.py:455
  32.7 0.6 %copy.12 = f32[1,4096]{1,0:T(1,128)} copy(f32[1,4096]{1,0:T(1,128)S(1)} %bitcast.6) | data formatting | bytes 32768
  33.3 0.6 %copy.13 = f32[2,4,1024]{2,1,0:T(4,128)} copy(f32[2,4,1024]{2,1,0:T(4,128)S(1)} %get-tuple-element.9) | data formatting | bytes 65536
Async XLA Ops:
  0.6 0.7 %copy-start.5 = (s32[8,1]{0,1:T(1,128)S(1)}, s32[8,1]{0,1:T(1,128)}, u32[]{:S(2)}) copy-start(s32[8,1]{0,1:T(1,128)} %param.10) | copy-start | bytes 100
  0.6 0.7 %copy-start.6 = (s32[8]{0:T(128)S(1)}, s32[8]{0:T(128)}, u32[]{:S(2)}) copy-start(s32[8]{0:T(128)} %offsets_ref.1) | copy-start | bytes 100
  0.7 0.7 %copy-start.7 = (f32[4]{0:T(128)S(1)}, f32[4]{0:T(128)}, u32[]{:S(2)}) copy-start(f32[4]{0:T(128)} %freq_ref.1) | copy-start | bytes 52
  1.3 0.9 %copy-start = (f32[4,8,1024]{2,1,0:T(8,128)S(1)}, f32[4,8,1024]{2,1,0:T(8,128)}, u32[]{:S(2)}) copy-start(f32[4,8,1024]{2,1,0:T(8,128)} %source_ref.1) | copy-start | bytes 393220
  2.2 0.9 %copy-start.1 = (f32[8,4096]{1,0:T(8,128)S(1)}, f32[8,4096]{1,0:T(8,128)}, u32[]{:S(2)}) copy-start(f32[8,4096]{1,0:T(8,128)} %traces_ref.1) | copy-start | bytes 393220
  3.1 0.8 %copy-start.2 = (f32[4,2,9,9]{3,1,2,0:T(2,128)S(1)}, f32[4,2,9,9]{3,1,2,0:T(2,128)}, u32[]{:S(2)}) copy-start(f32[4,2,9,9]{3,1,2,0:T(2,128)} %param.12) | copy-start | bytes 7780
  3.9 0.7 %copy-start.3 = (f32[1,4096]{1,0:T(1,128)S(1)}, f32[1,4096]{1,0:T(1,128)}, u32[]{:S(2)}) copy-start(f32[1,4096]{1,0:T(1,128)} %param.14) | copy-start | bytes 49156
  4.6 0.7 %copy-start.4 = (f32[1,4096]{1,0:T(1,128)S(1)}, f32[1,4096]{1,0:T(1,128)}, u32[]{:S(2)}) copy-start(f32[1,4096]{1,0:T(1,128)} %param.15) | copy-start | bytes 49156
